TPU v7x, 32 devices: a whole 2x2x4 slice. The times are simulated.
32 devices in a mesh: groups: 2 (over y), ep: 8 (over z, x), tp: 2 (over core).
Axes of the slice: x: 2, y: 2, z: 4, core: 2. Of those that a mesh axis runs over, the one named last changes fastest.
Arguments:
- residual: bfloat16 [512, 7168], P(('groups', 'ep'), 'tp'), parts along dimension 0
- attn_partial: bfloat16 [2, 512, 7168], P('tp', ('groups', 'ep')), parts along dimension 1, may hold values from -6 to 6
- norm_gain: float32 [7168], P('tp'), may hold values from 0.1 to 1.9
- route_ids: int32 [512, 8], P(('groups', 'ep')), parts along dimension 0, may hold values from 0 to 255, as said below
- route_scores: float32 [512, 8], P(('groups', 'ep')), parts along dimension 0, may hold values from 0.05 to 1
- w_in: bfloat16 [8, 7168, 4096], P('ep', 'tp'), may hold values from -0.0625 to 0.0625
- w_down: bfloat16 [8, 2048, 7168], P('ep', None, 'tp'), may hold values from -0.125 to 0.125
Outputs:
- stream: bfloat16 [512, 7168], P(('groups', 'ep'), 'tp'), parts along dimension 0
- moe_out: bfloat16 [512, 7168], P(('groups', 'ep'), 'tp'), parts along dimension 0
There are 2 independent parts, one for each index of `groups`. A program takes and returns all parts, laid end to end along the dimension named above; an argument that names none is the same for every part. Nothing has to cross between parts.
Inputs may be any that keep to these rules, and one draw needn't show every extreme that they name: `route_ids`: each row names 8 different experts. In each aligned block of 32 rows (the rows of one device) one expert below 8, the same in all blocks, is named by exactly 2 rows, and every other expert below 8 by exactly one row.
All inputs are finite; a program needn't handle non-finite values.
Results may differ from a plain program's by a relative error of at most 0.0076.
Values may be sent and summed in bfloat16 or wider, within the bound.
A program may use at most 320 MiB of HBM per device.

v0:
```python
import functools

import jax
import jax.numpy as jnp
from jax import lax
from jax.experimental import pallas as pl
from jax.experimental.pallas import tpu as pltpu
from jax.sharding import PartitionSpec as P

EXP = 8
CAP = 2
CH = 512
MESH = pl.DeviceIdType.MESH

route_scale = 2.5
norm_eps = 1e-06


def iota(shape, dim):
    return lax.broadcasted_iota(jnp.int32, shape, dim)


def each(count, body):
    if count <= 8:
        for step in range(count):
            body(step)
    else:

        def run(step, carry):
            body(step)
            return carry

        lax.fori_loop(0, count, run, 0)


def split_two(value):
    high = value.astype(jnp.bfloat16)
    return high, (value - high.astype(jnp.float32)).astype(jnp.bfloat16)


def route_tables(ids, scores, rows):
    wide = 8 * rows
    spread = (iota((rows, wide), 0) == (iota((rows, wide), 1) & (rows - 1))).astype(jnp.float32)
    turn = (((0,), (0,)), ((), ()))
    ids_t = lax.dot_general(
        ids.astype(jnp.float32).astype(jnp.bfloat16),
        spread.astype(jnp.bfloat16),
        turn,
        preferred_element_type=jnp.float32,
    )
    scores_t = lax.dot_general(
        scores,
        spread,
        turn,
        precision=lax.Precision.HIGHEST,
        preferred_element_type=jnp.float32,
    )
    shares = route_scale * scores_t / jnp.sum(scores_t, axis=0, keepdims=True)
    expert = iota((EXP, wide), 0).astype(jnp.float32)
    member = jnp.zeros((EXP, wide), jnp.float32)
    weight = jnp.zeros((EXP, wide), jnp.float32)
    for k in range(ids.shape[1]):
        hit = ids_t[k : k + 1, :] == expert
        member = jnp.where(hit, 1.0, member)
        weight = weight + jnp.where(hit, shares[k : k + 1, :], 0.0)
    earlier = iota((wide, wide), 0) < (iota((wide, wide), 1) & (rows - 1))
    rank = jnp.dot(
        member.astype(jnp.bfloat16),
        earlier.astype(jnp.float32).astype(jnp.bfloat16),
        preferred_element_type=jnp.float32,
    )
    code = jnp.where(member > 0.0, rank, -1.0)
    line = iota((16, wide), 0)
    same_chunk = (line >> 1) == (iota((16, wide), 1) // rows)
    want = jnp.where(same_chunk, (line & 1).astype(jnp.float32), -2.0)
    places, weighted = [], []
    for e in range(EXP):
        on = jnp.where(code[e : e + 1, :] == want, 1.0, 0.0)
        places.append(on)
        weighted.append(on * weight[e : e + 1, :])
    return jnp.concatenate(places, axis=0), jnp.concatenate(weighted, axis=0)


def kernel(
    ep,
    res_hbm, attn_hbm, gain_hbm, ids_hbm, scores_hbm, w_in_hbm, w_down_hbm,
    stream_hbm, moe_hbm,
    w_in, w_down, res, attn_own, attn_peer, gain, ids, scores,
    stream, moe, stacked, packed, recv, tokens, h_own, h_peer, sq_own, sq_peer,
    act, y_stack, y_packed, ret, weights_hi, weights_lo,
    in_sem, w_in_sem, w_down_sem, out_sem, tp_send, tp_recv,
    h_send, h_recv, go_send, go_recv, back_send, back_recv,
):
    rows, half = res.shape
    chunks = half // CH
    pieces = ep // EXP
    hidden = w_in.shape[1] // 2
    blocks, slots, _ = h_own.shape
    hb = hidden // blocks
    me = lax.axis_index("ep")
    core = lax.axis_index("tp")
    peer = 1 - core

    def local(src, dst, sem):
        copy = pltpu.make_async_copy(src, dst, sem)
        copy.start()
        return copy

    own_cols = pl.ds(pl.multiple_of(core * half, 128), half)
    peer_cols = pl.ds(pl.multiple_of(peer * half, 128), half)
    barrier = pltpu.get_barrier_semaphore()
    pl.semaphore_signal(barrier, inc=1, device_id={"tp": peer}, device_id_type=MESH)

    def greet(step):
        other = lax.rem(me + step + 1, ep)
        pl.semaphore_signal(barrier, inc=1, device_id={"ep": other}, device_id_type=MESH)

    each(ep - 1, greet)
    copy_ids = local(ids_hbm, ids, in_sem.at[0])
    copy_scores = local(scores_hbm, scores, in_sem.at[1])
    copy_attn = local(attn_hbm.at[0, :, own_cols], attn_own, in_sem.at[2])
    copy_res = local(res_hbm, res, in_sem.at[3])
    copy_gain = local(gain_hbm, gain, in_sem.at[4])
    copies_in, copies_down = [], []
    for b in range(blocks):
        for part in range(2):
            cols = pl.ds(part * hidden + b * hb, hb)
            copies_in.append(
                local(w_in_hbm.at[0, :, cols], w_in.at[:, cols], w_in_sem.at[2 * b + part])
            )
    for c in range(chunks):
        cols = pl.ds(c * CH, CH)
        copies_down.append(local(w_down_hbm.at[0, :, cols], w_down.at[:, cols], w_down_sem.at[c]))

    pl.semaphore_wait(barrier, ep)
    swap = pltpu.make_async_remote_copy(
        src_ref=attn_hbm.at[0, :, peer_cols],
        dst_ref=attn_peer,
        send_sem=tp_send.at[0],
        recv_sem=tp_recv.at[0],
        device_id={"tp": peer},
        device_id_type=MESH,
    )
    swap.start()

    copy_ids.wait()
    copy_scores.wait()
    place, weighted = route_tables(ids[...], scores[...], rows)
    weights_hi[...], weights_lo[...] = split_two(weighted.T)
    place = place.astype(jnp.bfloat16)
    side = iota((128, 128), 0)
    swapped = ((side & 14) << 3) | ((side >> 4) << 1) | (side & 1)
    shuffle = (swapped == iota((128, 128), 1)).astype(jnp.float32).astype(jnp.bfloat16)

    copy_attn.wait()
    copy_res.wait()
    copy_gain.wait()
    swap.wait()

    total = res[...].astype(jnp.float32) + (
        attn_own[...].astype(jnp.float32) + attn_peer[...].astype(jnp.float32)
    )
    stream[...] = total.astype(jnp.bfloat16)
    out_stream = local(stream, stream_hbm, out_sem.at[0])
    wide = stream[...].astype(jnp.float32)
    square = jnp.sum(wide * wide, axis=1, keepdims=True)
    scaled = wide * lax.rsqrt(square * (1.0 / half) + norm_eps) * gain[...]
    scaled = scaled.astype(jnp.bfloat16)
    for c in range(chunks):
        stacked[c * rows : (c + 1) * rows, :] = scaled[:, c * CH : (c + 1) * CH]
    square = jnp.minimum(square, 3.0e38)
    first = square.astype(jnp.bfloat16).astype(jnp.float32)
    second = (square - first).astype(jnp.bfloat16).astype(jnp.float32)
    third = square - first - second
    lane = iota((rows, CH), 1)
    terms = jnp.where(
        lane == 0, first, jnp.where(lane == 1, second, jnp.where(lane == 2, third, 0.0))
    )
    stacked[chunks * rows :, :] = terms.astype(jnp.bfloat16)
    sent = jnp.dot(place, stacked[...], preferred_element_type=jnp.float32)
    packed[...] = sent.astype(jnp.bfloat16).reshape(packed.shape)

    def go(step):
        other = lax.rem(me + step + 1, ep)
        return pltpu.make_async_remote_copy(
            src_ref=packed.at[other // pieces],
            dst_ref=recv.at[me],
            send_sem=go_send.at[other],
            recv_sem=go_recv.at[me],
            device_id={"ep": other},
            device_id_type=MESH,
        )

    def arrive(step):
        other = lax.rem(me + step + 1, ep)
        pltpu.make_async_remote_copy(
            src_ref=packed.at[0],
            dst_ref=recv.at[other],
            send_sem=go_send.at[other],
            recv_sem=go_recv.at[other],
            device_id={"ep": other},
            device_id_type=MESH,
        ).wait_recv()

    each(ep - 1, lambda step: go(step).start())
    recv[me] = packed[me // pieces]
    y_stack[:, chunks * 16 :, :] = jnp.zeros((ep // 8, 16, CH), jnp.bfloat16)
    each(ep - 1, arrive)

    for k in range(ep // 8):
        block = recv[8 * k : 8 * k + 8].reshape(128, CH)
        order = jnp.dot(shuffle, block, preferred_element_type=jnp.float32)
        for c in range(chunks):
            tokens[16 * k : 16 * k + 16, c * CH : (c + 1) * CH] = order[
                16 * c : 16 * c + 16
            ].astype(jnp.bfloat16)
        sums = jnp.sum(order[16 * chunks :], axis=1, keepdims=True)
        sq_own[16 * k : 16 * k + 16, :] = jnp.broadcast_to(sums, (16, 128))

    swap_sq = pltpu.make_async_remote_copy(
        src_ref=sq_own,
        dst_ref=sq_peer,
        send_sem=tp_send.at[1],
        recv_sem=tp_recv.at[1],
        device_id={"tp": peer},
        device_id_type=MESH,
    )
    swap_sq.start()

    swaps = []
    for b in range(blocks):
        for part in range(2):
            copies_in[2 * b + part].wait()
            cols = pl.ds(part * hidden + b * hb, hb)
            h_own[b, :, part * hb : (part + 1) * hb] = jnp.dot(
                tokens[...], w_in[:, cols], preferred_element_type=jnp.float32
            )
        swap_h = pltpu.make_async_remote_copy(
            src_ref=h_own.at[b],
            dst_ref=h_peer.at[b],
            send_sem=h_send.at[b],
            recv_sem=h_recv.at[b],
            device_id={"tp": peer},
            device_id_type=MESH,
        )
        swap_h.start()
        swaps.append(swap_h)

    swap_sq.wait()
    mean_own = sq_own[:, :1] * (1.0 / half)
    mean_peer = sq_peer[:, :1] * (1.0 / half)
    inverse = lax.rsqrt(0.5 * mean_own + 0.5 * mean_peer + norm_eps)
    scale_own = jnp.sqrt(mean_own + norm_eps) * inverse
    scale_peer = jnp.sqrt(mean_peer + norm_eps) * inverse
    for b in range(blocks):
        swaps[b].wait()
        both = scale_own * h_own[b] + scale_peer * h_peer[b]
        gate, up = both[:, :hb], both[:, hb:]
        act[:, b * hb : (b + 1) * hb] = (gate / (1.0 + jnp.exp(-gate)) * up).astype(jnp.bfloat16)

    for c in range(chunks):
        copies_down[c].wait()
        y = jnp.dot(
            act[...], w_down[:, c * CH : (c + 1) * CH], preferred_element_type=jnp.float32
        ).astype(jnp.bfloat16)
        for k in range(ep // 8):
            y_stack[k, 16 * c : 16 * c + 16, :] = y[16 * k : 16 * k + 16]
    for k in range(ep // 8):
        order = jnp.dot(shuffle, y_stack[k], preferred_element_type=jnp.float32)
        y_packed[8 * k : 8 * k + 8] = order.astype(jnp.bfloat16).reshape(8, 16, CH)

    def back(step):
        other = lax.rem(me + step + 1, ep)
        return pltpu.make_async_remote_copy(
            src_ref=y_packed.at[other],
            dst_ref=ret.at[me],
            send_sem=back_send.at[other],
            recv_sem=back_recv.at[me],
            device_id={"ep": other},
            device_id_type=MESH,
        )

    def return_arrive(step):
        other = lax.rem(me + step + 1, ep)
        pltpu.make_async_remote_copy(
            src_ref=y_packed.at[0],
            dst_ref=ret.at[other],
            send_sem=back_send.at[other],
            recv_sem=back_recv.at[other],
            device_id={"ep": other},
            device_id_type=MESH,
        ).wait_recv()

    each(ep - 1, lambda step: back(step).start())
    ret[me] = y_packed[me]
    each(ep - 1, lambda step: go(step).wait_send())
    each(ep - 1, return_arrive)

    def combine(s):
        if pieces == 1:
            part = ret[...].reshape(EXP * 16, CH)
        else:
            part = jnp.concatenate([ret[e * pieces + s] for e in range(EXP)], axis=0)
        return jnp.dot(
            weights_hi[...], part, preferred_element_type=jnp.float32
        ) + jnp.dot(weights_lo[...], part, preferred_element_type=jnp.float32)

    result = combine(0)
    if pieces > 1:
        result = lax.fori_loop(1, pieces, lambda s, running: running + combine(s), result)
    for c in range(chunks):
        moe[:, c * CH : (c + 1) * CH] = result[c * rows : (c + 1) * rows].astype(jnp.bfloat16)
    out_moe = local(moe, moe_hbm, out_sem.at[1])
    each(ep - 1, lambda step: back(step).wait_send())
    out_stream.wait()
    out_moe.wait()


def per_device(residual, attn_partial, norm_gain, route_ids, route_scores, w_in, w_down):
    rows, half = residual.shape
    hidden = w_in.shape[2] // 2
    ep = lax.axis_size("ep")
    slots = ep * CAP
    hb = min(512, hidden)
    blocks = hidden // hb
    chunks = half // CH
    bf16, f32 = jnp.bfloat16, jnp.float32
    dma = pltpu.SemaphoreType.DMA
    anywhere = pl.BlockSpec(memory_space=pl.ANY)
    scratch = [
        pltpu.VMEM(w_in.shape[1:], bf16),
        pltpu.VMEM(w_down.shape[1:], bf16),
        pltpu.VMEM((rows, half), bf16),
        pltpu.VMEM((rows, half), bf16),
        pltpu.VMEM((rows, half), bf16),
        pltpu.VMEM((1, half), f32),
        pltpu.VMEM(route_ids.shape, jnp.int32),
        pltpu.VMEM(route_scores.shape, f32),
        pltpu.VMEM((rows, half), bf16),
        pltpu.VMEM((rows, half), bf16),
        pltpu.VMEM((8 * rows, CH), bf16),
        pltpu.VMEM((EXP, 16, CH), bf16),
        pltpu.VMEM((ep, 16, CH), bf16),
        pltpu.VMEM((slots, half), bf16),
        pltpu.VMEM((blocks, slots, 2 * hb), f32),
        pltpu.VMEM((blocks, slots, 2 * hb), f32),
        pltpu.VMEM((slots, 128), f32),
        pltpu.VMEM((slots, 128), f32),
        pltpu.VMEM((slots, hidden), bf16),
        pltpu.VMEM((ep // 8, 128, CH), bf16),
        pltpu.VMEM((ep, 16, CH), bf16),
        pltpu.VMEM((ep, 16, CH), bf16),
        pltpu.VMEM((8 * rows, EXP * 16), bf16),
        pltpu.VMEM((8 * rows, EXP * 16), bf16),
        dma((5,)),
        dma((2 * blocks,)),
        dma((chunks,)),
        dma((2,)),
        dma((2,)),
        dma((2,)),
        dma((blocks,)),
        dma((blocks,)),
        dma((ep,)),
        dma((ep,)),
        dma((ep,)),
        dma((ep,)),
    ]
    return pl.pallas_call(
        functools.partial(kernel, ep),
        out_shape=(
            jax.ShapeDtypeStruct((rows, half), bf16),
            jax.ShapeDtypeStruct((rows, half), bf16),
        ),
        in_specs=[anywhere] * 7,
        out_specs=(anywhere, anywhere),
        scratch_shapes=scratch,
        compiler_params=pltpu.CompilerParams(
            collective_id=0, has_side_effects=True, vmem_limit_bytes=56 * 1024 * 1024
        ),
        cost_estimate=pl.CostEstimate(
            flops=2 * slots * (w_in.size + w_down.size),
            bytes_accessed=2 * (w_in.size + w_down.size),
            transcendentals=slots * hidden,
        ),
    )(residual, attn_partial, norm_gain.reshape(1, half), route_ids, route_scores, w_in, w_down)


def solution(mesh):
    in_specs = (
        P(("groups", "ep"), "tp"),
        P("tp", ("groups", "ep"), None),
        P("tp"),
        P(("groups", "ep"), None),
        P(("groups", "ep"), None),
        P("ep", "tp", None),
        P("ep", None, "tp"),
    )
    out_specs = (P(("groups", "ep"), "tp"), P(("groups", "ep"), "tp"))
    return jax.shard_map(
        per_device, mesh=mesh, in_specs=in_specs, out_specs=out_specs, check_vma=False
    )
```

profile of v0, /device:TPU:0, one launch (start us, length us, event | category | flops | bytes accessed | tf_op | source)
XLA Modules:
  0.0 43.2 jit_solution(2381158090922175793)
XLA Ops:
  0.6 1.3 %reshape.7.gain_hbm = f32[1,3584]{1,0:T(1,128)} reshape(f32[3584]{0:T(1024)} %param.9) | data formatting | bytes 28672 | tf_op jit(solution)/shard_map/reshape | solution.py:385
  2.0 1.4 %copy.9.ids_hbm = s32[32,8]{1,0:T(8,128)} copy(s32[32,8]{0,1:T(8,128)} %param.10) | data formatting | bytes 2048 | tf_op args[3]
  3.3 1.4 %copy.10.scores_hbm = f32[32,8]{1,0:T(8,128)} copy(f32[32,8]{0,1:T(8,128)} %param.11) | data formatting | bytes 2048 | tf_op args[4]
  4.7 35.2 %shard_map.86 = (bf16[32,3584]{1,0:T(8,128)(2,1)}, bf16[32,3584]{1,0:T(8,128)(2,1)}) custom-call(bf16[32,3584]{1,0:T(8,128)(2,1)} %res_hbm.1, bf16[1,32,7168]{2,1,0:T(8,128)(2,1)} %attn_hbm.1, f32[1,3584]{1,0:T(1,128)} %reshape.7.gain_hbm, s32[32,8]{1,0:T(8,128)} %copy.9.ids_hbm, f32[32,8]{1,0:T(8,128)} %copy.10.scores_hbm, bf16[1,3584,4096]{2,1,0:T(8,128)(2,1)} %w_in_hbm.1, ...), custom_call_target="tpu_custom_call" | custom-call | flops 704643072 | bytes 44040192 | tf_op jit(solution)/shard_map/pallas_call | solution.py:368
  39.9 1.6 %copy.13 = bf16[32,3584]{1,0:T(8,128)(2,1)} copy(bf16[32,3584]{1,0:T(8,128)(2,1)} %get-tuple-element.4) | data formatting | bytes 458752
  41.6 1.6 %copy.14 = bf16[32,3584]{1,0:T(8,128)(2,1)} copy(bf16[32,3584]{1,0:T(8,128)(2,1)} %get-tuple-element.5) | data formatting | bytes 458752
where the time goes:
time: 43.5 us; the launch traced here: 43.2 us
  Pallas kernels  35.2 us (81%)
  local copies, waits for them, and re-layouts  7.34 us (17%)
  between operations  0.64 us (1%)
    pallas_call x1, Pallas kernels, per_device(): pl.pallas_call(functools.partial(kernel, ep), out_shape=(jax.ShapeDtypeSt...  35.2 us
    unnamed x4, local copies, waits for them, and re-layouts  6.01 us
    reshape x1, local copies, waits for them, and re-layouts, per_device(): norm_gain.reshape(1, half)  1.32 us

commit v1 on v0

--- a/solution.py
+++ b/solution.py
@@ -10,6 +10,7 @@
 EXP = 8
 CAP = 2
 CH = 512
+IN_CUTS = 8
 MESH = pl.DeviceIdType.MESH
 
 route_scale = 2.5
@@ -41,17 +42,14 @@
 def route_tables(ids, scores, rows):
     wide = 8 * rows
     spread = (iota((rows, wide), 0) == (iota((rows, wide), 1) & (rows - 1))).astype(jnp.float32)
-    turn = (((0,), (0,)), ((), ()))
-    ids_t = lax.dot_general(
+    ids_t = jnp.dot(
         ids.astype(jnp.float32).astype(jnp.bfloat16),
         spread.astype(jnp.bfloat16),
-        turn,
         preferred_element_type=jnp.float32,
     )
-    scores_t = lax.dot_general(
+    scores_t = jnp.dot(
         scores,
         spread,
-        turn,
         precision=lax.Precision.HIGHEST,
         preferred_element_type=jnp.float32,
     )
@@ -59,7 +57,7 @@
     expert = iota((EXP, wide), 0).astype(jnp.float32)
     member = jnp.zeros((EXP, wide), jnp.float32)
     weight = jnp.zeros((EXP, wide), jnp.float32)
-    for k in range(ids.shape[1]):
+    for k in range(ids.shape[0]):
         hit = ids_t[k : k + 1, :] == expert
         member = jnp.where(hit, 1.0, member)
         weight = weight + jnp.where(hit, shares[k : k + 1, :], 0.0)
@@ -84,10 +82,10 @@
 def kernel(
     ep,
     res_hbm, attn_hbm, gain_hbm, ids_hbm, scores_hbm, w_in_hbm, w_down_hbm,
-    stream_hbm, moe_hbm,
+    stream_hbm, ret, hi_hbm, lo_hbm,
     w_in, w_down, res, attn_own, attn_peer, gain, ids, scores,
-    stream, moe, stacked, packed, recv, tokens, h_own, h_peer, sq_own, sq_peer,
-    act, y_stack, y_packed, ret, weights_hi, weights_lo,
+    stream, stacked, packed, recv, tokens, h_own, h_peer, sq_own, sq_peer,
+    running, y_stack, y_packed, weights_hi, weights_lo,
     in_sem, w_in_sem, w_down_sem, out_sem, tp_send, tp_recv,
     h_send, h_recv, go_send, go_recv, back_send, back_recv,
 ):
@@ -122,15 +120,22 @@
     copy_res = local(res_hbm, res, in_sem.at[3])
     copy_gain = local(gain_hbm, gain, in_sem.at[4])
     copies_in, copies_down = [], []
-    for b in range(blocks):
-        for part in range(2):
-            cols = pl.ds(part * hidden + b * hb, hb)
-            copies_in.append(
-                local(w_in_hbm.at[0, :, cols], w_in.at[:, cols], w_in_sem.at[2 * b + part])
-            )
-    for c in range(chunks):
-        cols = pl.ds(c * CH, CH)
-        copies_down.append(local(w_down_hbm.at[0, :, cols], w_down.at[:, cols], w_down_sem.at[c]))
+
+    def start_down():
+        for k in range(blocks):
+            part = pl.ds(k * hb, hb)
+            copies_down.append(local(w_down_hbm.at[0, part], w_down.at[part], w_down_sem.at[k]))
+
+    copy_ids.wait()
+    copy_scores.wait()
+    place, weighted = route_tables(ids[...], scores[...], rows)
+    weights_hi[...], weights_lo[...] = split_two(weighted.T)
+    out_hi = local(weights_hi, hi_hbm, out_sem.at[1])
+    out_lo = local(weights_lo, lo_hbm, out_sem.at[2])
+    place = place.astype(jnp.bfloat16)
+    side = iota((128, 128), 0)
+    swapped = ((side & 14) << 3) | ((side >> 4) << 1) | (side & 1)
+    shuffle = (swapped == iota((128, 128), 1)).astype(jnp.float32).astype(jnp.bfloat16)
 
     pl.semaphore_wait(barrier, ep)
     swap = pltpu.make_async_remote_copy(
@@ -143,15 +148,9 @@
     )
     swap.start()
 
-    copy_ids.wait()
-    copy_scores.wait()
-    place, weighted = route_tables(ids[...], scores[...], rows)
-    weights_hi[...], weights_lo[...] = split_two(weighted.T)
-    place = place.astype(jnp.bfloat16)
-    side = iota((128, 128), 0)
-    swapped = ((side & 14) << 3) | ((side >> 4) << 1) | (side & 1)
-    shuffle = (swapped == iota((128, 128), 1)).astype(jnp.float32).astype(jnp.bfloat16)
-
+    for k in range(IN_CUTS):
+        part = pl.ds(k * (half // IN_CUTS), half // IN_CUTS)
+        copies_in.append(local(w_in_hbm.at[0, part], w_in.at[part], w_in_sem.at[k]))
     copy_attn.wait()
     copy_res.wait()
     copy_gain.wait()
@@ -164,10 +163,12 @@
     out_stream = local(stream, stream_hbm, out_sem.at[0])
     wide = stream[...].astype(jnp.float32)
     square = jnp.sum(wide * wide, axis=1, keepdims=True)
-    scaled = wide * lax.rsqrt(square * (1.0 / half) + norm_eps) * gain[...]
-    scaled = scaled.astype(jnp.bfloat16)
-    for c in range(chunks):
-        stacked[c * rows : (c + 1) * rows, :] = scaled[:, c * CH : (c + 1) * CH]
+    scaled = wide * lax.rsqrt(square * (1.0 / half) + norm_eps)
+    for j in range(half // 128):
+        c, at = divmod(j * 128, CH)
+        stacked[c * rows : (c + 1) * rows, at : at + 128] = (
+            scaled[:, j * 128 : (j + 1) * 128] * gain[j : j + 1, :]
+        ).astype(jnp.bfloat16)
     square = jnp.minimum(square, 3.0e38)
     first = square.astype(jnp.bfloat16).astype(jnp.float32)
     second = (square - first).astype(jnp.bfloat16).astype(jnp.float32)
@@ -203,6 +204,7 @@
         ).wait_recv()
 
     each(ep - 1, lambda step: go(step).start())
+    start_down()
     recv[me] = packed[me // pieces]
     y_stack[:, chunks * 16 :, :] = jnp.zeros((ep // 8, 16, CH), jnp.bfloat16)
     each(ep - 1, arrive)
@@ -228,9 +230,10 @@
     swap_sq.start()
 
     swaps = []
+    for copy in copies_in:
+        copy.wait()
     for b in range(blocks):
         for part in range(2):
-            copies_in[2 * b + part].wait()
             cols = pl.ds(part * hidden + b * hb, hb)
             h_own[b, :, part * hb : (part + 1) * hb] = jnp.dot(
                 tokens[...], w_in[:, cols], preferred_element_type=jnp.float32
@@ -256,15 +259,21 @@
         swaps[b].wait()
         both = scale_own * h_own[b] + scale_peer * h_peer[b]
         gate, up = both[:, :hb], both[:, hb:]
-        act[:, b * hb : (b + 1) * hb] = (gate / (1.0 + jnp.exp(-gate)) * up).astype(jnp.bfloat16)
-
-    for c in range(chunks):
-        copies_down[c].wait()
-        y = jnp.dot(
-            act[...], w_down[:, c * CH : (c + 1) * CH], preferred_element_type=jnp.float32
-        ).astype(jnp.bfloat16)
-        for k in range(ep // 8):
-            y_stack[k, 16 * c : 16 * c + 16, :] = y[16 * k : 16 * k + 16]
+        active = (gate / (1.0 + jnp.exp(-gate)) * up).astype(jnp.bfloat16)
+        copies_down[b].wait()
+        for c in range(chunks):
+            cols = slice(c * CH, (c + 1) * CH)
+            y = jnp.dot(
+                active, w_down[b * hb : (b + 1) * hb, cols], preferred_element_type=jnp.float32
+            )
+            if b > 0:
+                y = y + running[:, cols]
+            if b < blocks - 1:
+                running[:, cols] = y
+                continue
+            y = y.astype(jnp.bfloat16)
+            for k in range(ep // 8):
+                y_stack[k, 16 * c : 16 * c + 16, :] = y[16 * k : 16 * k + 16]
     for k in range(ep // 8):
         order = jnp.dot(shuffle, y_stack[k], preferred_element_type=jnp.float32)
         y_packed[8 * k : 8 * k + 8] = order.astype(jnp.bfloat16).reshape(8, 16, CH)
@@ -292,9 +301,34 @@
         ).wait_recv()
 
     each(ep - 1, lambda step: back(step).start())
-    ret[me] = y_packed[me]
+    own_back = local(y_packed.at[me], ret.at[me], out_sem.at[3])
     each(ep - 1, lambda step: go(step).wait_send())
     each(ep - 1, return_arrive)
+
+    each(ep - 1, lambda step: back(step).wait_send())
+    own_back.wait()
+    out_stream.wait()
+    out_hi.wait()
+    out_lo.wait()
+
+
+def combine_kernel(
+    pieces,
+    stream_in, ret_hbm, hi_hbm, lo_hbm, stream_out, moe_hbm, stream, ret, hi, lo, moe, sem,
+):
+    rows, half = moe.shape
+    pairs = (
+        (stream_in, stream), (ret_hbm, ret), (hi_hbm, hi), (lo_hbm, lo),
+    )
+    copies = []
+    for place, (src, dst) in enumerate(pairs):
+        copies.append(pltpu.make_async_copy(src, dst, sem.at[place]))
+        copies[-1].start()
+    copies[0].wait()
+    out_stream = pltpu.make_async_copy(stream, stream_out, sem.at[len(pairs) + 1])
+    out_stream.start()
+    for copy in copies[1:]:
+        copy.wait()
 
     def combine(s):
         if pieces == 1:
@@ -302,18 +336,18 @@
         else:
             part = jnp.concatenate([ret[e * pieces + s] for e in range(EXP)], axis=0)
         return jnp.dot(
-            weights_hi[...], part, preferred_element_type=jnp.float32
-        ) + jnp.dot(weights_lo[...], part, preferred_element_type=jnp.float32)
+            hi[...], part, preferred_element_type=jnp.float32
+        ) + jnp.dot(lo[...], part, preferred_element_type=jnp.float32)
 
     result = combine(0)
     if pieces > 1:
         result = lax.fori_loop(1, pieces, lambda s, running: running + combine(s), result)
-    for c in range(chunks):
+    for c in range(half // CH):
         moe[:, c * CH : (c + 1) * CH] = result[c * rows : (c + 1) * rows].astype(jnp.bfloat16)
-    out_moe = local(moe, moe_hbm, out_sem.at[1])
-    each(ep - 1, lambda step: back(step).wait_send())
+    out = pltpu.make_async_copy(moe, moe_hbm, sem.at[len(pairs)])
+    out.start()
     out_stream.wait()
-    out_moe.wait()
+    out.wait()
 
 
 def per_device(residual, attn_partial, norm_gain, route_ids, route_scores, w_in, w_down):
@@ -333,10 +367,9 @@
         pltpu.VMEM((rows, half), bf16),
         pltpu.VMEM((rows, half), bf16),
         pltpu.VMEM((rows, half), bf16),
-        pltpu.VMEM((1, half), f32),
-        pltpu.VMEM(route_ids.shape, jnp.int32),
-        pltpu.VMEM(route_scores.shape, f32),
-        pltpu.VMEM((rows, half), bf16),
+        pltpu.VMEM((half // 128, 128), f32),
+        pltpu.VMEM(route_ids.shape[::-1], jnp.int32),
+        pltpu.VMEM(route_scores.shape[::-1], f32),
         pltpu.VMEM((rows, half), bf16),
         pltpu.VMEM((8 * rows, CH), bf16),
         pltpu.VMEM((EXP, 16, CH), bf16),
@@ -346,16 +379,15 @@
         pltpu.VMEM((blocks, slots, 2 * hb), f32),
         pltpu.VMEM((slots, 128), f32),
         pltpu.VMEM((slots, 128), f32),
-        pltpu.VMEM((slots, hidden), bf16),
+        pltpu.VMEM((slots, half), f32),
         pltpu.VMEM((ep // 8, 128, CH), bf16),
-        pltpu.VMEM((ep, 16, CH), bf16),
         pltpu.VMEM((ep, 16, CH), bf16),
         pltpu.VMEM((8 * rows, EXP * 16), bf16),
         pltpu.VMEM((8 * rows, EXP * 16), bf16),
         dma((5,)),
-        dma((2 * blocks,)),
-        dma((chunks,)),
-        dma((2,)),
+        dma((IN_CUTS,)),
+        dma((blocks,)),
+        dma((4,)),
         dma((2,)),
         dma((2,)),
         dma((blocks,)),
@@ -365,14 +397,17 @@
         dma((ep,)),
         dma((ep,)),
     ]
-    return pl.pallas_call(
+    weights_shape = (8 * rows, EXP * 16)
+    stream, ret, high, low = pl.pallas_call(
         functools.partial(kernel, ep),
         out_shape=(
             jax.ShapeDtypeStruct((rows, half), bf16),
-            jax.ShapeDtypeStruct((rows, half), bf16),
+            jax.ShapeDtypeStruct((ep, 16, CH), bf16),
+            jax.ShapeDtypeStruct(weights_shape, bf16),
+            jax.ShapeDtypeStruct(weights_shape, bf16),
         ),
         in_specs=[anywhere] * 7,
-        out_specs=(anywhere, anywhere),
+        out_specs=(anywhere,) * 4,
         scratch_shapes=scratch,
         compiler_params=pltpu.CompilerParams(
             collective_id=0, has_side_effects=True, vmem_limit_bytes=56 * 1024 * 1024
@@ -382,7 +417,35 @@
             bytes_accessed=2 * (w_in.size + w_down.size),
             transcendentals=slots * hidden,
         ),
-    )(residual, attn_partial, norm_gain.reshape(1, half), route_ids, route_scores, w_in, w_down)
+    )(
+        residual,
+        attn_partial,
+        norm_gain.reshape(half // 128, 128),
+        route_ids.T,
+        route_scores.T,
+        w_in,
+        w_down,
+    )
+    return pl.pallas_call(
+        functools.partial(combine_kernel, ep // EXP),
+        out_shape=(
+            jax.ShapeDtypeStruct((rows, half), bf16),
+            jax.ShapeDtypeStruct((rows, half), bf16),
+        ),
+        in_specs=[anywhere] * 4,
+        out_specs=(anywhere, anywhere),
+        scratch_shapes=[
+            pltpu.VMEM((rows, half), bf16),
+            pltpu.VMEM((ep, 16, CH), bf16),
+            pltpu.VMEM(weights_shape, bf16),
+            pltpu.VMEM(weights_shape, bf16),
+            pltpu.VMEM((rows, half), bf16),
+            dma((6,)),
+        ],
+        cost_estimate=pl.CostEstimate(
+            flops=4 * 8 * rows * ep * 16 * CH, bytes_accessed=8 * rows * half, transcendentals=0
+        ),
+    )(stream, ret, high, low)
 
 
 def solution(mesh):

time: 43.5 us -> 29 us (0.67)
  local copies, waits for them, and re-layouts: 7.34 us -> 0 us
  Pallas kernels: 35.2 us -> 28.1 us
    pallas_call x1, Pallas kernels: 35.2 us -> 26.1 us  [per_device(): pl.pallas_call(functools.partial(kernel, ep), out_shape=(jax.ShapeDtypeSt...]
    unnamed x4 -> x0, local copies, waits for them, and re-layouts: 6.01 us -> none
    pallas_call x0 -> x1, Pallas kernels: none -> 2.05 us  [per_device(): pl.pallas_call(functools.partial(combine_kernel, ep // EXP), out_shape=(j...]
    reshape x1 -> x0, local copies, waits for them, and re-layouts: 1.32 us -> none  [per_device(): norm_gain.reshape(1, half)]
where the time goes in v1:
time: 29 us; the launch traced here: 28.8 us
  Pallas kernels  28.1 us (97%)
  between operations  0.64 us (2%)
    pallas_call x1, Pallas kernels, per_device(): pl.pallas_call(functools.partial(kernel, ep), out_shape=(jax.ShapeDtypeSt...  26.1 us
    pallas_call x1, Pallas kernels, per_device(): pl.pallas_call(functools.partial(combine_kernel, ep // EXP), out_shape=(j...  2.05 us

profile of v1, /device:TPU:0, one launch (start us, length us, event | category | flops | bytes accessed | tf_op | source)
XLA Modules:
  0.0 28.8 jit_solution(17000664407496302142)
XLA Ops:
  0.6 26.1 %shard_map.86 = (bf16[32,3584]{1,0:T(8,128)(2,1)}, bf16[8,16,512]{2,1,0:T(8,128)(2,1)}, bf16[256,128]{1,0:T(8,128)(2,1)}, bf16[256,128]{1,0:T(8,128)(2,1)}) custom-call(bf16[32,3584]{1,0:T(8,128)(2,1)} %res_hbm.1, bf16[1,32,7168]{2,1,0:T(8,128)(2,1)} %attn_hbm.1, f32[28,128]{1,0:T(8,128)} %bitcast.3, s32[8,32]{1,0:T(8,128)} %bitcast.4, f32[8,32]{1,0:T(8,128)} %bitcast.5, ...), custom_call_target="tpu_custom_call" | custom-call | flops 704643072 | bytes 44040192 | tf_op jit(solution)/shard_map/pallas_call | solution.py:401
  26.7 2.1 %shard_map.87 = (bf16[32,3584]{1,0:T(8,128)(2,1)}, bf16[32,3584]{1,0:T(8,128)(2,1)}) custom-call(bf16[32,3584]{1,0:T(8,128)(2,1)} %get-tuple-element.6.stream_in, bf16[8,16,512]{2,1,0:T(8,128)(2,1)} %get-tuple-element.7.ret_hbm, bf16[256,128]{1,0:T(8,128)(2,1)} %get-tuple-element.8.hi_hbm, bf16[256,128]{1,0:T(8,128)(2,1)} %get-tuple-element.9.lo_hbm), custom_call_target="tpu_custom_call" | custom-call | flops 67108864 | bytes 917504 | tf_op jit(solution)/shard_map/pallas_call | solution.py:429

commit v2 on v1

--- a/solution.py
+++ b/solution.py
@@ -11,6 +11,7 @@
 CAP = 2
 CH = 512
 IN_CUTS = 8
+EARLY = 4
 MESH = pl.DeviceIdType.MESH
 
 route_scale = 2.5
@@ -121,11 +122,17 @@
     copy_gain = local(gain_hbm, gain, in_sem.at[4])
     copies_in, copies_down = [], []
 
+    def start_in(first, last):
+        for k in range(first, last):
+            part = pl.ds(k * (half // IN_CUTS), half // IN_CUTS)
+            copies_in.append(local(w_in_hbm.at[0, part], w_in.at[part], w_in_sem.at[k]))
+
     def start_down():
         for k in range(blocks):
             part = pl.ds(k * hb, hb)
             copies_down.append(local(w_down_hbm.at[0, part], w_down.at[part], w_down_sem.at[k]))
 
+    start_in(0, EARLY)
     copy_ids.wait()
     copy_scores.wait()
     place, weighted = route_tables(ids[...], scores[...], rows)
@@ -148,9 +155,7 @@
     )
     swap.start()
 
-    for k in range(IN_CUTS):
-        part = pl.ds(k * (half // IN_CUTS), half // IN_CUTS)
-        copies_in.append(local(w_in_hbm.at[0, part], w_in.at[part], w_in_sem.at[k]))
+    start_in(EARLY, IN_CUTS)
     copy_attn.wait()
     copy_res.wait()
     copy_gain.wait()
@@ -314,21 +319,11 @@
 
 def combine_kernel(
     pieces,
-    stream_in, ret_hbm, hi_hbm, lo_hbm, stream_out, moe_hbm, stream, ret, hi, lo, moe, sem,
+    stream, ret, hi, lo, stream_out, moe_hbm, moe, sem,
 ):
     rows, half = moe.shape
-    pairs = (
-        (stream_in, stream), (ret_hbm, ret), (hi_hbm, hi), (lo_hbm, lo),
-    )
-    copies = []
-    for place, (src, dst) in enumerate(pairs):
-        copies.append(pltpu.make_async_copy(src, dst, sem.at[place]))
-        copies[-1].start()
-    copies[0].wait()
-    out_stream = pltpu.make_async_copy(stream, stream_out, sem.at[len(pairs) + 1])
+    out_stream = pltpu.make_async_copy(stream, stream_out, sem.at[0])
     out_stream.start()
-    for copy in copies[1:]:
-        copy.wait()
 
     def combine(s):
         if pieces == 1:
@@ -344,7 +339,7 @@
         result = lax.fori_loop(1, pieces, lambda s, running: running + combine(s), result)
     for c in range(half // CH):
         moe[:, c * CH : (c + 1) * CH] = result[c * rows : (c + 1) * rows].astype(jnp.bfloat16)
-    out = pltpu.make_async_copy(moe, moe_hbm, sem.at[len(pairs)])
+    out = pltpu.make_async_copy(moe, moe_hbm, sem.at[1])
     out.start()
     out_stream.wait()
     out.wait()
@@ -406,11 +401,11 @@
             jax.ShapeDtypeStruct(weights_shape, bf16),
             jax.ShapeDtypeStruct(weights_shape, bf16),
         ),
-        in_specs=[anywhere] * 7,
+        in_specs=[pl.BlockSpec(memory_space=pltpu.HBM)] * 7,
         out_specs=(anywhere,) * 4,
         scratch_shapes=scratch,
         compiler_params=pltpu.CompilerParams(
-            collective_id=0, has_side_effects=True, vmem_limit_bytes=56 * 1024 * 1024
+            collective_id=0, has_side_effects=True, vmem_limit_bytes=48 * 1024 * 1024
         ),
         cost_estimate=pl.CostEstimate(
             flops=2 * slots * (w_in.size + w_down.size),
@@ -418,13 +413,18 @@
             transcendentals=slots * hidden,
         ),
     )(
-        residual,
-        attn_partial,
-        norm_gain.reshape(half // 128, 128),
-        route_ids.T,
-        route_scores.T,
-        w_in,
-        w_down,
+        *(
+            pltpu.with_memory_space_constraint(operand, pltpu.HBM)
+            for operand in (
+                residual,
+                attn_partial,
+                norm_gain.reshape(half // 128, 128),
+                route_ids.T,
+                route_scores.T,
+                w_in,
+                w_down,
+            )
+        )
     )
     return pl.pallas_call(
         functools.partial(combine_kernel, ep // EXP),
@@ -432,16 +432,10 @@
             jax.ShapeDtypeStruct((rows, half), bf16),
             jax.ShapeDtypeStruct((rows, half), bf16),
         ),
-        in_specs=[anywhere] * 4,
-        out_specs=(anywhere, anywhere),
-        scratch_shapes=[
-            pltpu.VMEM((rows, half), bf16),
-            pltpu.VMEM((ep, 16, CH), bf16),
-            pltpu.VMEM(weights_shape, bf16),
-            pltpu.VMEM(weights_shape, bf16),
-            pltpu.VMEM((rows, half), bf16),
-            dma((6,)),
-        ],
+        in_specs=[pl.BlockSpec(memory_space=pltpu.VMEM)] * 4,
+        out_specs=(pl.BlockSpec(memory_space=pltpu.HBM),) * 2,
+        scratch_shapes=[pltpu.VMEM((rows, half), bf16), dma((2,))],
+        compiler_params=pltpu.CompilerParams(vmem_limit_bytes=4 * 1024 * 1024),
         cost_estimate=pl.CostEstimate(
             flops=4 * 8 * rows * ep * 16 * CH, bytes_accessed=8 * rows * half, transcendentals=0
         ),

time: 29 us -> 27.2 us (0.938)
  Pallas kernels: 28.1 us -> 26.4 us
    pallas_call x1, Pallas kernels: 2.05 us -> 0.98 us  [per_device(): pl.pallas_call(functools.partial(combine_kernel, ep // EXP), out_shape=(j...]
    pallas_call x1, Pallas kernels: 26.1 us -> 25.4 us  [per_device(): pl.pallas_call(functools.partial(kernel, ep), out_shape=(jax.ShapeDtypeSt...]
where the time goes in v2:
time: 27.2 us; the launch traced here: 27 us
  Pallas kernels  26.4 us (97%)
  between operations  0.64 us (2%)
    pallas_call x1, Pallas kernels, per_device(): pl.pallas_call(functools.partial(kernel, ep), out_shape=(jax.ShapeDtypeSt...  25.4 us
    pallas_call x1, Pallas kernels, per_device(): pl.pallas_call(functools.partial(combine_kernel, ep // EXP), out_shape=(j...  0.98 us

profile of v2, /device:TPU:0, one launch (start us, length us, event | category | flops | bytes accessed | tf_op | source)
XLA Modules:
  0.0 27.0 jit_solution(17324496244642335341)
XLA Ops:
  0.6 25.4 %shard_map.86 = (bf16[32,3584]{1,0:T(8,128)(2,1)S(1)}, bf16[8,16,512]{2,1,0:T(8,128)(2,1)S(1)}, bf16[256,128]{1,0:T(8,128)(2,1)S(1)}, bf16[256,128]{1,0:T(8,128)(2,1)S(1)}) custom-call(bf16[32,3584]{1,0:T(8,128)(2,1)} %res_hbm.1, bf16[1,32,7168]{2,1,0:T(8,128)(2,1)} %attn_hbm.1, f32[28,128]{1,0:T(8,128)} %bitcast.3, s32[8,32]{1,0:T(8,128)} %bitcast.4, ...), custom_call_target="tpu_custom_call" | custom-call | flops 704643072 | bytes 44040192 | tf_op jit(solution)/shard_map/pallas_call | solution.py:396
  26.0 1.0 %shard_map.87 = (bf16[32,3584]{1,0:T(8,128)(2,1)}, bf16[32,3584]{1,0:T(8,128)(2,1)}) custom-call(bf16[32,3584]{1,0:T(8,128)(2,1)S(1)} %get-tuple-element.6.stream, bf16[8,16,512]{2,1,0:T(8,128)(2,1)S(1)} %get-tuple-element.7.ret, bf16[256,128]{1,0:T(8,128)(2,1)S(1)} %get-tuple-element.8.hi, bf16[256,128]{1,0:T(8,128)(2,1)S(1)} %get-tuple-element.9.lo), custom_call_target="tpu_custom_call" | custom-call | flops 67108864 | bytes 917504 | tf_op jit(solution)/shard_map/pallas_call | solution.py:429
